TPU v7x, 256 devices: a whole 4x4x8 slice. The times are simulated.
256 devices in a mesh: code: 128 (over y, z, x_lo, core), dp: 2 (over x_hi).
Axes of the slice: x: 4 (x_hi: 2, x_lo: 2; x = x_hi * 2 + x_lo), y: 4, z: 8, core: 2. Of those that a mesh axis runs over, the one named last changes fastest.
Arguments:
- latents: bfloat16 [2, 4096, 256], P('dp', 'code'), may hold values from -24 to 24
- codebook: bfloat16 [131072, 256], P('code'), may hold values from -0.7 to 0.7
- cotangent: bfloat16 [2, 4096, 256], P('dp', 'code'), may hold values from -6 to 6
Outputs:
- quantized: bfloat16 [2, 4096, 256], P('dp', 'code')
- code_grad: float32 [131072, 256], P('code')
All inputs are finite; a program needn't handle non-finite values.
Results may differ from a plain program's by a relative error of at most 0.0095.
Values may be sent and summed in bfloat16 or wider, within the bound.
A program may use at most 128 MiB of HBM per device.

v0:
```python
import jax
import jax.numpy as jnp
from jax import lax
from jax.sharding import PartitionSpec as P


def shard_grad(rows_lat, rows_cot, block, top, total, inner):
    by_feature = (((1,), (1,)), ((), ()))
    by_token = (((0,), (0,)), ((), ()))
    block_f32 = block.astype(jnp.float32)
    half = 0.5 * jnp.sum(block_f32 * block_f32, axis=1)
    scores = (
        lax.dot_general(rows_lat, block, by_feature, preferred_element_type=jnp.float32)
        - half[None, :]
    )
    prob = jnp.exp(scores - top[:, None]) / total[:, None]
    align = lax.dot_general(rows_cot, block, by_feature, preferred_element_type=jnp.float32)
    slope = prob * (align - inner[:, None])
    first = lax.dot_general(
        prob.astype(jnp.bfloat16), rows_cot, by_token, preferred_element_type=jnp.float32
    )
    second = lax.dot_general(
        slope.astype(jnp.bfloat16), rows_lat, by_token, preferred_element_type=jnp.float32
    )
    return first + second - jnp.sum(slope, axis=0)[:, None] * block_f32


def body(latents, codebook, cotangent):
    own_lat = latents[0]
    own_cot = cotangent[0]
    all_lat, all_cot = (
        lax.all_gather(own_lat, "code", axis=0, tiled=True),
        lax.all_gather(own_cot, "code", axis=0, tiled=True),
    )
    code_f32 = codebook.astype(jnp.float32)
    half_norm = 0.5 * jnp.sum(code_f32 * code_f32, axis=1)
    by_feature = (((1,), (1,)), ((), ()))
    logits = (
        lax.dot_general(all_lat, codebook, by_feature, preferred_element_type=jnp.float32)
        - half_norm[None, :]
    )
    top = lax.pmax(jnp.max(logits, axis=1), "code")
    expo = jnp.exp(logits - top[:, None])
    total = lax.psum(jnp.sum(expo, axis=1), "code")
    weights = expo.astype(jnp.bfloat16)
    own_rows = own_lat.shape[0]
    own_start = lax.axis_index("code") * own_rows
    own_mixed = lax.psum_scatter(
        jnp.dot(weights, codebook, preferred_element_type=jnp.float32),
        "code",
        scatter_dimension=0,
        tiled=True,
    )
    own_total = lax.dynamic_slice_in_dim(total, own_start, own_rows, 0)
    own_quant = own_mixed / own_total[:, None]
    own_inner = jnp.sum(own_cot.astype(jnp.float32) * own_quant, axis=1)
    inner = lax.all_gather(own_inner, "code", axis=0, tiled=True)
    scale = (
        codebook.shape[0] * lax.axis_size("code") * 1.0 / (lax.axis_size("dp") * all_lat.shape[0])
    )
    local_grad = shard_grad(all_lat, all_cot, codebook, top, total, inner)
    summed = lax.psum(local_grad.astype(jnp.bfloat16), "dp").astype(jnp.float32)
    return (own_quant.astype(jnp.bfloat16)[None], summed * scale)


def solution(mesh):
    in_specs = (P("dp", "code", None), P("code", None), P("dp", "code", None))
    out_specs = (P("dp", "code", None), P("code", None))
    return jax.shard_map(body, mesh=mesh, in_specs=in_specs, out_specs=out_specs, check_vma=False)
```

profile of v0, /device:TPU:1, one launch (start us, length us, event | category | flops | bytes accessed | tf_op | source)
XLA Modules:
  0.0 1975.4 jit_solution(12623658902980179050)
XLA Ops:
  7.2 0.0 copy-start.1
  7.2 0.0 all-gather.5.cloned.1.call-start
  7.2 0.7 all-gather.5.cloned.1.call-update
  7.9 0.0 reduce-scatter.2.cloned.1.call-start
  8.0 1.3 fusion.31
  9.2 216.8 %all-gather.5.cloned.1.call-done = bf16[1,4096,256]{2,1,0:T(8,128)(2,1)} async-done(((bf16[1,32,256]{2,1,0:T(8,128)(2,1)}), bf16[1,4096,256]{2,1,0:T(8,128)(2,1)}) %all-gather.5.cloned.1.call-update) | async-done | bytes 2097168 | tf_op jit(solution)/shard_map/all_gather | solution.py:32
  226.0 9.8 subtract_reduce_fusion
  235.7 544.7 %pmax.7 = f32[4096]{0:T(1024)S(1)} all-reduce(f32[4096]{0:T(1024)S(1)} %get-tuple-element.4), channel_id=1, replica_groups=mesh['code'=128,'dp'=2] {'code'}, use_global_device_ids=true, to_apply=%region_2.0 | all-reduce | flops 4096 | bytes 32768 | tf_op jit(solution)/shard_map/pmax | solution.py:42
  780.5 0.0 copy-done.1
  780.5 0.0 copy-start.4
  780.5 11.1 fusion.3
  791.6 0.0 copy-start.2
  791.6 0.0 reduce-scatter.2.cloned.1.call-update
  791.6 0.0 all-gather.7.cloned.1.call-start
  791.7 0.7 all-gather.7.cloned.1.call-update
  792.4 0.0 all-reduce.3.cloned.1.call-start
  792.4 0.0 copy-done.4
  792.4 0.6 dynamic-slice
  793.7 9.3 fusion.1
  802.9 548.7 %psum.14 = f32[4096]{0:T(1024)S(1)} all-reduce(f32[4096]{0:T(1024)S(1)} %fusion.1), channel_id=1, replica_groups=mesh['code'=128,'dp'=2] {'code'}, use_global_device_ids=true, to_apply=%region_5.0 | all-reduce | flops 4096 | bytes 32768 | tf_op jit(solution)/shard_map/psum | solution.py:44
  1351.7 0.1 dynamic_slice.3
  1351.7 2.8 reduce-scatter.2.cloned.1.call-done
  1354.6 0.0 copy-done.2
  1354.6 1.5 fusion.32
  1356.1 0.3 dynamic-update-slice
  1356.4 548.6 %all-reduce = f32[4096]{0:T(1024)S(1)} all-reduce(f32[4096]{0:T(1024)S(1)} %dynamic-update-slice), channel_id=1, replica_groups=mesh['code'=128,'dp'=2] {'code'}, use_global_device_ids=true, to_apply=%add | all-reduce | flops 4096 | bytes 32768
  1905.0 0.0 copy-start
  1905.0 0.0 all-gather.7.cloned.1.call-done
  1905.0 0.0 copy-start.3
  1905.0 9.9 fusion.34
  1915.0 0.0 copy-done
  1915.0 2.4 fusion.5
  1917.3 0.0 copy-done.3
  1917.3 8.3 fusion.26
  1925.7 0.0 all-reduce.3.cloned.1.call-update
  1925.7 41.1 %all-reduce.3.cloned.1.call-done = bf16[1024,256]{1,0:T(8,128)(2,1)} async-done(((bf16[1024,256]{1,0:T(8,128)(2,1)}), bf16[1024,256]{1,0:T(8,128)(2,1)}) %all-reduce.3.cloned.1.call-update) | async-done | bytes 524304 | tf_op jit(solution)/shard_map/psum | solution.py:62
  1966.8 2.1 convert_multiply_fusion.2
  (2 shorter events, 0.0 us)
Async XLA Ops:
  7.2 773.3 %copy-start.1 = (bf16[1024,256]{1,0:T(8,128)(2,1)S(1)}, bf16[1024,256]{1,0:T(8,128)(2,1)}, u32[]{:S(2)}) copy-start(bf16[1024,256]{1,0:T(8,128)(2,1)} %param.4) | copy-start | bytes 1572868
  7.2 218.8 %all-gather.5.cloned.1.call-start = ((), (), s32[]{:S(2)}) async-start(), calls=%async_computation.3 | async-start | bytes 2113536 | tf_op jit(solution)/shard_map/all_gather | solution.py:32
  7.9 1346.7 %reduce-scatter.2.cloned.1.call-start = ((), (), s32[]{:S(2)}) async-start(), calls=%async_computation.1 | async-start | bytes 4227072 | tf_op jit(solution)/shard_map/reduce_scatter | solution.py:48
  780.5 12.0 copy-start.4
  791.6 563.0 %copy-start.2 = (bf16[1,32,256]{2,1,0:T(8,128)(2,1)S(1)}, bf16[1,32,256]{2,1,0:T(8,128)(2,1)}, u32[]{:S(2)}) copy-start(bf16[1,32,256]{2,1,0:T(8,128)(2,1)} %param.5) | copy-start | bytes 49156
  791.6 1113.4 %all-gather.7.cloned.1.call-start = ((), (), s32[]{:S(2)}) async-start(), calls=%async_computation.4 | async-start | bytes 2113536 | tf_op jit(solution)/shard_map/all_gather | solution.py:33
  792.4 1174.4 %all-reduce.3.cloned.1.call-start = ((), (), s32[]{:S(2)}) async-start(), calls=%async_computation.2 | async-start | bytes 1048576 | tf_op jit(solution)/shard_map/psum | solution.py:62
  1905.0 9.9 copy-start
  1905.0 12.3 copy-start.3
Sparse Core Ops, SparseCore 0:
  9.9 216.0 all-gather.4
  791.8 562.7 reduce-scatter.1
  1356.6 211.3 all-gather.6
  1925.8 40.9 all-reduce.2
where the time goes:
time: 1980 us
  blocking collectives  1640 us (83%)
  waiting for transfers between devices  262 us (13%)
  matrix products  41.5 us (2%)
    psum x1, blocking collectives, body(): total = lax.psum(jnp.sum(expo, axis=1), 'code')  549 us
    unnamed x1, blocking collectives  549 us
    pmax x1, blocking collectives, body(): top = lax.pmax(jnp.max(logits, axis=1), 'code')  545 us
    all_gather x1, waiting for transfers between devices, body(): lax.all_gather(own_lat, 'code', axis=0, tiled=True)  217 us
    psum x1, waiting for transfers between devices, body(): summed = lax.psum(local_grad.astype(jnp.bfloat16), 'dp').astype(jnp.float32)  41.1 us
  transfers between devices with their start and end apart: 4, of which 3 were waited for; matrix products, arithmetic and copies ran while one was open for 1% of the time, Pallas kernels for 0%

commit v1 on v0

--- a/solution.py
+++ b/solution.py
@@ -41,7 +41,7 @@
     )
     top = lax.pmax(jnp.max(logits, axis=1), "code")
     expo = jnp.exp(logits - top[:, None])
-    total = lax.psum(jnp.sum(expo, axis=1), "code")
+    total = jnp.sum(lax.all_gather(jnp.sum(expo, axis=1), "code"), axis=0)
     weights = expo.astype(jnp.bfloat16)
     own_rows = own_lat.shape[0]
     own_start = lax.axis_index("code") * own_rows

time: 1980 us -> 2190 us (1.11)
  waiting for transfers between devices: 262 us -> 1020 us
  blocking collectives: 1640 us -> 1090 us
    reduce_scatter x1, waiting for transfers between devices: 2.84 us -> 563 us  [body(): lax.psum_scatter(jnp.dot(weights, codebook, preferred_element_type=jnp.fl...]
    psum x1 -> x0, blocking collectives: 549 us -> none  [body(): total = lax.psum(jnp.sum(expo, axis=1), 'code')]
    all_gather x0 -> x1, waiting for transfers between devices: none -> 199 us  [body(): total = jnp.sum(lax.all_gather(jnp.sum(expo, axis=1), 'code'), axis=0)]
  transfers between devices with their start and end apart: 4 -> 5, of which waited for: 3 -> 4; matrix products, arithmetic and copies ran while one was open for 1% -> 1% of each run, Pallas kernels for 0% -> 0%
where the time goes in v1:
time: 2190 us
  blocking collectives  1090 us (50%)
  waiting for transfers between devices  1020 us (47%)
  matrix products  41.5 us (2%)
    reduce_scatter x1, waiting for transfers between devices, body(): lax.psum_scatter(jnp.dot(weights, codebook, preferred_element_type=jnp.fl...  563 us
    unnamed x1, blocking collectives  549 us
    pmax x1, blocking collectives, body(): top = lax.pmax(jnp.max(logits, axis=1), 'code')  545 us
    all_gather x1, waiting for transfers between devices, body(): lax.all_gather(own_lat, 'code', axis=0, tiled=True)  217 us
    all_gather x1, waiting for transfers between devices, body(): total = jnp.sum(lax.all_gather(jnp.sum(expo, axis=1), 'code'), axis=0)  199 us
  transfers between devices with their start and end apart: 5, of which 4 were waited for; matrix products, arithmetic and copies ran while one was open for 1% of the time, Pallas kernels for 0%

profile of v1, /device:TPU:1, one launch (start us, length us, event | category | flops | bytes accessed | tf_op | source)
XLA Modules:
  0.0 2187.9 jit_solution(16599337899348708162)
XLA Ops:
  7.2 0.0 all-gather.7.cloned.1.call-start
  7.2 0.7 all-gather.7.cloned.1.call-update
  7.9 0.0 all-gather.9.cloned.1.call-start
  7.9 1.3 fusion.31
  9.2 0.0 copy-start.1
  9.2 216.7 %all-gather.7.cloned.1.call-done = bf16[1,4096,256]{2,1,0:T(8,128)(2,1)} async-done(((bf16[1,32,256]{2,1,0:T(8,128)(2,1)}), bf16[1,4096,256]{2,1,0:T(8,128)(2,1)}) %all-gather.7.cloned.1.call-update) | async-done | bytes 2097168 | tf_op jit(solution)/shard_map/all_gather | solution.py:32
  226.0 9.8 subtract_reduce_fusion
  235.7 544.7 %pmax.7 = f32[4096]{0:T(1024)S(1)} all-reduce(f32[4096]{0:T(1024)S(1)} %get-tuple-element.4), channel_id=1, replica_groups=mesh['code'=128,'dp'=2] {'code'}, use_global_device_ids=true, to_apply=%region_2.0 | all-reduce | flops 4096 | bytes 32768 | tf_op jit(solution)/shard_map/pmax | solution.py:42
  780.4 9.9 fusion.1
  790.3 0.0 all-gather.9.cloned.1.call-update
  790.3 0.0 copy-start.4
  790.3 0.0 copy-start.2
  790.3 0.0 reduce-scatter.2.cloned.1.call-start
  790.4 0.0 copy-done.1
  790.4 11.1 fusion.3
  801.5 0.0 reduce-scatter.2.cloned.1.call-update
  801.6 0.0 all-gather.11.cloned.1.call-start
  801.6 0.5 all-gather.11.cloned.1.call-update
  802.1 0.0 all-reduce.3.cloned.1.call-start
  802.2 0.0 copy-done.4
  802.2 0.6 dynamic-slice
  803.4 198.8 %all-gather.9.cloned.1.call-done = f32[524288]{0:T(1024)} async-done(((f32[4096]{0:T(1024)}), f32[524288]{0:T(1024)}) %all-gather.9.cloned.1.call-update) | async-done | bytes 2097168 | tf_op jit(solution)/shard_map/all_gather | solution.py:44
  1002.3 1.7 reshape.13
  1004.0 0.1 reduce_sum.51
  1004.2 0.1 dynamic_slice.3
  1004.2 562.7 %reduce-scatter.2.cloned.1.call-done = f32[32,256]{1,0:T(8,128)} async-done(((f32[4096,256]{1,0:T(8,128)}), f32[32,256]{1,0:T(8,128)}) %reduce-scatter.2.cloned.1.call-update) | async-done | bytes 32784 | tf_op jit(solution)/shard_map/reduce_scatter | solution.py:48
  1566.9 0.0 copy-done.2
  1566.9 1.5 fusion.32
  1568.5 0.3 dynamic-update-slice
  1568.8 548.6 %all-reduce = f32[4096]{0:T(1024)S(1)} all-reduce(f32[4096]{0:T(1024)S(1)} %dynamic-update-slice), channel_id=1, replica_groups=mesh['code'=128,'dp'=2] {'code'}, use_global_device_ids=true, to_apply=%add | all-reduce | flops 4096 | bytes 32768
  2117.4 0.0 copy-start
  2117.4 0.0 all-gather.11.cloned.1.call-done
  2117.4 0.0 copy-start.3
  2117.4 9.9 fusion.34
  2127.3 0.0 copy-done
  2127.3 2.4 fusion.5
  2129.7 0.0 copy-done.3
  2129.7 8.4 fusion.26
  2138.1 0.0 all-reduce.3.cloned.1.call-update
  2138.1 41.2 %all-reduce.3.cloned.1.call-done = bf16[1024,256]{1,0:T(8,128)(2,1)} async-done(((bf16[1024,256]{1,0:T(8,128)(2,1)}), bf16[1024,256]{1,0:T(8,128)(2,1)}) %all-reduce.3.cloned.1.call-update) | async-done | bytes 524304 | tf_op jit(solution)/shard_map/psum | solution.py:62
  2179.3 2.1 convert_multiply_fusion.2
  (2 shorter events, 0.0 us)
Async XLA Ops:
  7.2 218.8 %all-gather.7.cloned.1.call-start = ((), (), s32[]{:S(2)}) async-start(), calls=%async_computation.3 | async-start | bytes 2113536 | tf_op jit(solution)/shard_map/all_gather | solution.py:32
  7.9 994.4 %all-gather.9.cloned.1.call-start = ((), (), s32[]{:S(2)}) async-start(), calls=%async_computation.4 | async-start | bytes 2113536 | tf_op jit(solution)/shard_map/all_gather | solution.py:44
  9.2 781.2 %copy-start.1 = (bf16[1024,256]{1,0:T(8,128)(2,1)S(1)}, bf16[1024,256]{1,0:T(8,128)(2,1)}, u32[]{:S(2)}) copy-start(bf16[1024,256]{1,0:T(8,128)(2,1)} %param.4) | copy-start | bytes 1572868
  790.3 11.9 copy-start.4
  790.3 776.6 %copy-start.2 = (bf16[1,32,256]{2,1,0:T(8,128)(2,1)S(1)}, bf16[1,32,256]{2,1,0:T(8,128)(2,1)}, u32[]{:S(2)}) copy-start(bf16[1,32,256]{2,1,0:T(8,128)(2,1)} %param.5) | copy-start | bytes 49156
  790.3 776.6 %reduce-scatter.2.cloned.1.call-start = ((), (), s32[]{:S(2)}) async-start(), calls=%async_computation.1 | async-start | bytes 4227072 | tf_op jit(solution)/shard_map/reduce_scatter | solution.py:48
  801.6 1315.9 %all-gather.11.cloned.1.call-start = ((), (), s32[]{:S(2)}) async-start(), calls=%async_computation.5 | async-start | bytes 2113536 | tf_op jit(solution)/shard_map/all_gather | solution.py:33
  802.1 1377.2 %all-reduce.3.cloned.1.call-start = ((), (), s32[]{:S(2)}) async-start(), calls=%async_computation.2 | async-start | bytes 1048576 | tf_op jit(solution)/shard_map/psum | solution.py:62
  2117.4 9.9 copy-start
  2117.4 12.3 copy-start.3
Sparse Core Ops, SparseCore 0:
  9.9 216.0 all-gather.6
  790.4 211.7 all-gather.8
  1004.8 562.1 reduce-scatter.1
  1568.8 211.4 all-gather.10
  2138.2 41.0 all-reduce.2

commit v2 on v0

--- a/solution.py
+++ b/solution.py
@@ -29,7 +29,9 @@
     own_lat = latents[0]
     own_cot = cotangent[0]
     all_lat, all_cot = (
-        lax.all_gather(own_lat, "code", axis=0, tiled=True),
+        jnp.concatenate(
+            lax.all_to_all(jnp.stack([own_lat] * lax.axis_size("code")), "code", 0, 0), axis=0
+        ),
         lax.all_gather(own_cot, "code", axis=0, tiled=True),
     )
     code_f32 = codebook.astype(jnp.float32)

time: 1980 us -> 1830 us (0.924)
  waiting for transfers between devices: 262 us -> 93.1 us
    all_gather x1 -> x0, waiting for transfers between devices: 217 us -> none  [body(): lax.all_gather(own_lat, 'code', axis=0, tiled=True)]
    all_to_all x0 -> x1, waiting for transfers between devices: none -> 48.9 us  [body(): lax.all_to_all(jnp.stack([own_lat] * lax.axis_size('code')), 'code', 0, 0)]
where the time goes in v2:
time: 1830 us; the launch traced here: 1820 us
  blocking collectives  1640 us (90%)
  waiting for transfers between devices  93.1 us (5%)
  matrix products  42.8 us (2%)
    psum x1, blocking collectives, body(): total = lax.psum(jnp.sum(expo, axis=1), 'code')  549 us
    unnamed x1, blocking collectives  548 us
    pmax x1, blocking collectives, body(): top = lax.pmax(jnp.max(logits, axis=1), 'code')  544 us
    all_to_all x1, waiting for transfers between devices, body(): lax.all_to_all(jnp.stack([own_lat] * lax.axis_size('code')), 'code', 0, 0)  48.9 us
    psum x1, waiting for transfers between devices, body(): summed = lax.psum(local_grad.astype(jnp.bfloat16), 'dp').astype(jnp.float32)  41.4 us
  transfers between devices with their start and end apart: 4, of which 3 were waited for; matrix products, arithmetic and copies ran while one was open for 1% of the time, Pallas kernels for 0%

profile of v2, /device:TPU:1, one launch (start us, length us, event | category | flops | bytes accessed | tf_op | source)
XLA Modules:
  0.0 1824.8 jit_solution(12024335891545679257)
XLA Ops:
  7.2 0.0 copy-start
  7.2 2.4 stack.3
  9.6 14.9 all-to-all-start
  24.4 0.0 reduce-scatter.2.cloned.1.call-start
  24.5 1.3 fusion.28
  25.8 48.9 %all-to-all-done = bf16[128,32,256]{2,1,0:T(8,128)(2,1)S(1)} async-done(((bf16[128,32,256]{2,1,0:T(8,128)(2,1)}), bf16[128,32,256]{2,1,0:T(8,128)(2,1)S(1)}, u32[]{:S(2)}, u32[]{:S(2)}) %all-to-all-start) | async-done | bytes 2097184 | tf_op jit(solution)/shard_map/all_to_all | solution.py:33
  74.6 9.1 subtract_reduce_fusion
  83.8 544.4 %pmax.7 = f32[4096]{0:T(1024)S(1)} all-reduce(f32[4096]{0:T(1024)S(1)} %get-tuple-element.4), channel_id=1, replica_groups=mesh['code'=128,'dp'=2] {'code'}, use_global_device_ids=true, to_apply=%region_2.0 | all-reduce | flops 4096 | bytes 32768 | tf_op jit(solution)/shard_map/pmax | solution.py:44
  628.2 0.0 copy-done
  628.2 0.0 copy-start.3
  628.2 11.1 fusion.3
  639.3 0.0 copy-start.1
  639.3 0.0 reduce-scatter.2.cloned.1.call-update
  639.3 0.0 all-gather.3.cloned.1.call-start
  639.4 0.7 all-gather.3.cloned.1.call-update
  640.1 0.2 all-reduce.3.cloned.1.call-start
  640.3 0.0 copy-done.3
  640.3 0.6 dynamic-slice
  641.6 9.3 fusion.1
  650.8 548.8 %psum.14 = f32[4096]{0:T(1024)S(1)} all-reduce(f32[4096]{0:T(1024)S(1)} %fusion.1), channel_id=1, replica_groups=mesh['code'=128,'dp'=2] {'code'}, use_global_device_ids=true, to_apply=%region_5.0 | all-reduce | flops 4096 | bytes 32768 | tf_op jit(solution)/shard_map/psum | solution.py:46
  1199.6 0.1 dynamic_slice.3
  1199.7 2.1 reduce-scatter.2.cloned.1.call-done
  1201.8 0.0 copy-done.1
  1201.8 1.5 fusion.29
  1203.4 0.3 dynamic-update-slice
  1203.7 548.5 %all-reduce = f32[4096]{0:T(1024)S(1)} all-reduce(f32[4096]{0:T(1024)S(1)} %dynamic-update-slice), channel_id=1, replica_groups=mesh['code'=128,'dp'=2] {'code'}, use_global_device_ids=true, to_apply=%add | all-reduce | flops 4096 | bytes 32768
  1752.1 0.0 all-gather.3.cloned.1.call-done
  1752.1 0.0 copy-start.2
  1752.1 11.9 fusion.31
  1764.0 2.3 fusion.5
  1766.4 0.0 copy-done.2
  1766.4 8.3 fusion.23
  1774.7 0.0 all-reduce.3.cloned.1.call-update
  1774.8 41.4 %all-reduce.3.cloned.1.call-done = bf16[1024,256]{1,0:T(8,128)(2,1)} async-done(((bf16[1024,256]{1,0:T(8,128)(2,1)}), bf16[1024,256]{1,0:T(8,128)(2,1)}) %all-reduce.3.cloned.1.call-update) | async-done | bytes 524304 | tf_op jit(solution)/shard_map/psum | solution.py:64
  1816.2 2.1 convert_multiply_fusion.2
  (2 shorter events, 0.0 us)
Async XLA Ops:
  7.2 621.0 %copy-start = (bf16[1024,256]{1,0:T(8,128)(2,1)S(1)}, bf16[1024,256]{1,0:T(8,128)(2,1)}, u32[]{:S(2)}) copy-start(bf16[1024,256]{1,0:T(8,128)(2,1)} %param.4) | copy-start | bytes 1572868
  9.6 65.0 %all-to-all-start = ((bf16[128,32,256]{2,1,0:T(8,128)(2,1)}), bf16[128,32,256]{2,1,0:T(8,128)(2,1)S(1)}, u32[]{:S(2)}, u32[]{:S(2)}) async-start(bf16[128,32,256]{2,1,0:T(8,128)(2,1)} %stack.3), calls=%async_computation | async-start | bytes 4194304 | tf_op jit(solution)/shard_map/all_to_all | solution.py:33
  24.4 1177.4 %reduce-scatter.2.cloned.1.call-start = ((), (), s32[]{:S(2)}) async-start(), calls=%async_computation.2 | async-start | bytes 4227072 | tf_op jit(solution)/shard_map/reduce_scatter | solution.py:50
  628.2 12.2 copy-start.3
  639.3 562.5 %copy-start.1 = (bf16[1,32,256]{2,1,0:T(8,128)(2,1)S(1)}, bf16[1,32,256]{2,1,0:T(8,128)(2,1)}, u32[]{:S(2)}) copy-start(bf16[1,32,256]{2,1,0:T(8,128)(2,1)} %param.5) | copy-start | bytes 49156
  639.3 1112.8 %all-gather.3.cloned.1.call-start = ((), (), s32[]{:S(2)}) async-start(), calls=%async_computation.4 | async-start | bytes 2113536 | tf_op jit(solution)/shard_map/all_gather | solution.py:35
  640.1 1176.1 %all-reduce.3.cloned.1.call-start = ((), (), s32[]{:S(2)}) async-start(), calls=%async_computation.3 | async-start | bytes 1048576 | tf_op jit(solution)/shard_map/psum | solution.py:64
  1752.1 14.3 copy-start.2
Sparse Core Ops, SparseCore 0:
  639.5 562.3 reduce-scatter.1
  1203.8 211.8 all-gather.2
  1774.9 41.2 all-reduce.2
